TPU v7x, 128 devices: a whole 4x4x4 slice. The times are simulated.
128 devices in a mesh: row: 8 (over z, x_hi), col: 16 (over y, x_lo, core).
Axes of the slice: x: 4 (x_hi: 2, x_lo: 2; x = x_hi * 2 + x_lo), y: 4, z: 4, core: 2. Of those that a mesh axis runs over, the one named last changes fastest.
Arguments:
- residual: float32 [6144, 64000], P('row', 'col'), may hold values from -6 to 6
- cycle_coupling: float32 [6144, 1, 768], P('row', None, 'col'), may hold values from -0.21875 to 0.21875
- pair_amps: float32 [80, 614400], P(None, ('row', 'col')), may hold values from -6 to 6
- occupied_order: int32 [80], replicated, may hold values from 0 to 79, each once
- virtual_order: int32 [800], replicated, may hold values from 0 to 799, each once
Outputs:
- residual_out: float32 [6144, 64000], P('row', 'col')
Inputs may be any that keep to these rules, and one draw needn't show every extreme that they name: `occupied_order`: every canonical occupied orbital appears once. `virtual_order`: every canonical virtual orbital appears once.
All inputs are finite; a program needn't handle non-finite values.
Results may differ from a plain program's by a relative error of at most 0.000051.
Values sent between devices are 32-bit elements; how exact they have to be, the bound alone decides.
A program may use at most 192 MiB of HBM per device.

v0:
```python
import jax
import jax.numpy as jnp
from jax import lax
from jax.sharding import PartitionSpec as P


def inverse_of(order):
    length = order.shape[0]
    return jnp.zeros((length,), jnp.int32).at[order].set(jnp.arange(length, dtype=jnp.int32))


def contract_block(coupling, block):
    return jnp.einsum(
        "rkc,kjcb->rjb",
        coupling,
        block,
        precision=lax.Precision.HIGHEST,
        preferred_element_type=jnp.float32,
    )


def shards(residual, cycle_coupling, pair_amps, occupied_order, virtual_order):
    occupied = occupied_order.shape[0]
    virtual = virtual_order.shape[0]
    panel_orbitals = cycle_coupling.shape[1]
    local_rows = residual.shape[0]
    occupied_inverse = inverse_of(occupied_order)
    virtual_inverse = inverse_of(virtual_order)
    stored = pair_amps.reshape(panel_orbitals, occupied, pair_amps.shape[1] // virtual, virtual)
    stored = jnp.take(stored, occupied_inverse, axis=1)
    coupling = lax.all_gather(cycle_coupling, "col", axis=2, tiled=True)
    across = lax.all_gather(stored, "row", axis=2, tiled=True)
    regrouped = lax.all_to_all(across, "col", split_axis=1, concat_axis=2, tiled=True)
    regrouped = jnp.take(regrouped, virtual_inverse, axis=3)
    rows_count = lax.axis_size("row")
    cols_count = lax.axis_size("col")
    block_width = stored.shape[2]
    reordered = coupling.reshape(local_rows, panel_orbitals, rows_count, cols_count, block_width)
    reordered = reordered.transpose(0, 1, 3, 2, 4).reshape(
        local_rows, panel_orbitals, rows_count * cols_count * block_width
    )
    update = contract_block(reordered, regrouped)
    return residual + update.reshape(local_rows, update.shape[1] * virtual)


def solution(mesh):
    in_specs = (P("row", "col"), P("row", None, "col"), P(None, ("row", "col")), P(), P())
    out_specs = P("row", "col")
    return jax.shard_map(shards, mesh=mesh, in_specs=in_specs, out_specs=out_specs, check_vma=False)
```

profile of v0, /device:TPU:24, one launch (start us, length us, event | category | flops | bytes accessed | tf_op | source)
XLA Modules:
  0.0 483.1 jit_solution(12727276632947013641)
XLA Ops:
  7.4 0.0 all-gather.3.cloned.1.call-start
  7.4 0.7 compare_select_fusion.3
  8.0 0.8 scatter_custom_fusion.1
  8.9 3.2 reshape.38
  12.1 2.3 gather_fusion
  14.4 0.3 bitcast_select_fusion
  14.7 1.5 copy.10
  16.2 0.0 all-gather.3.cloned.1.call-update
  16.2 158.0 %all-gather.3.cloned.1.call-done = f32[1,80,48,800]{3,1,0,2:T(8,128)} async-done(((f32[1,80,6,800]{3,1,0,2:T(8,128)}), f32[1,80,48,800]{3,1,0,2:T(8,128)}) %all-gather.3.cloned.1.call-update) | async-done | bytes 12288016 | tf_op jit(solution)/shard_map/all_gather | solution.py:32
  174.3 14.3 %copy.11 = f32[1,80,48,800]{3,2,0,1:T(8,128)} copy(f32[1,80,48,800]{3,1,0,2:T(8,128)} %all-gather.3.cloned.1.call-done) | data formatting | bytes 24576000 | tf_op jit(solution)/shard_map/all_gather | solution.py:32
  188.6 0.0 copy-start.1
  188.6 5.4 %all-to-all-start = ((f32[1,80,48,800]{3,2,0,1:T(8,128)}), f32[1,80,48,800]{3,2,0,1:T(8,128)}, u32[]{:S(2)}, u32[]{:S(2)}) async-start(f32[1,80,48,800]{3,2,0,1:T(8,128)} %copy.11), calls=%async_computation | async-start | bytes 27525120 | tf_op jit(solution)/shard_map/all_to_all | solution.py:33
  194.0 0.0 all-gather.5.cloned.1.call-start
  194.0 0.5 all-gather.5.cloned.1.call-update
  194.6 0.0 copy-done.1
  194.6 5.5 %scatter_custom_fusion = s32[800]{0:T(1024)S(1)} fusion(s32[800]{0:T(1024)S(1)} %compare_select_fusion.1, s32[800]{0:T(1024)S(1)} %iota.6, s32[]{:T(128)} %constant.18.clone.1), kind=kCustom, calls=%fused_computation.14 | custom fusion | bytes 3204 | tf_op jit(solution)/shard_map/scatter | solution.py:9
  200.1 163.5 %all-gather.5.cloned.1.call-done = f32[768,1,768]{0,2,1:T(8,128)} async-done(((f32[768,1,48]{0,2,1:T(8,128)}), f32[768,1,768]{0,2,1:T(8,128)}) %all-gather.5.cloned.1.call-update) | async-done | bytes 2359312 | tf_op jit(solution)/shard_map/all_gather | solution.py:31
  363.6 4.5 reshape.36
  368.1 2.1 copy.15
  370.2 1.6 reshape.37
  371.8 0.0 all-to-all-done
  371.8 11.0 %copy.12 = f32[1,16,5,48,800]{4,3,1,2,0:T(8,128)} copy(f32[1,16,5,48,800]{4,3,2,1,0:T(8,128)} %bitcast.1) | data formatting | bytes 24576000 | tf_op jit(solution)/shard_map/all_to_all | solution.py:33
  382.8 18.5 %copy.13 = f32[5,768,800]{1,0,2:T(8,128)} copy(f32[5,768,800]{2,1,0:T(8,128)} %bitcast.19) | data formatting | bytes 24576000 | tf_op jit(solution)/shard_map/all_to_all | solution.py:33
  401.4 27.5 %gather_fusion.1 = f32[800,5,768]{2,1,0:T(8,128)} fusion(f32[5,768,800]{1,0,2:T(8,128)} %copy.13, s32[1024]{0:T(1024)S(1)} %pad_clamp_fusion), kind=kCustom, calls=%fused_computation.1 | custom fusion | bytes 24579200 | tf_op jit(solution)/shard_map/jit(_take)/gather | solution.py:34
  428.9 8.7 %select_bitcast_fusion = f32[5,800,768]{2,0,1:T(8,128)S(1)} fusion(f32[800,5,768]{2,1,0:T(8,128)} %gather_fusion.1, pred[800]{0:T(1024)(128)(4,1)S(1)} %compare_and_fusion), kind=kLoop, calls=%fused_computation.4 | loop fusion | flops 3072000 | bytes 24576800 | tf_op jit(solution)/shard_map/rkc,kjcb->rjb/dot_general | solution.py:13
  437.5 0.0 copy-start
  437.6 4.0 copy.14
  441.5 0.0 copy-done
  441.5 34.1 %bitcast_add_fusion = f32[768,4000]{0,1:T(8,128)} fusion(f32[768,4000]{0,1:T(8,128)} %param.5, f32[4000,768]{1,0:T(8,128)S(1)} %bitcast.18, f32[768,768]{0,1:T(8,128)S(1)} %copy-done), kind=kOutput, calls=%fused_computation.5 | convolution fusion | flops 28314624000 | bytes 39223296 | tf_op jit(solution)/shard_map/rkc,kjcb->rjb/dot_general | solution.py:13
  (9 shorter events, 0.0 us)
Async XLA Ops:
  7.4 166.9 %all-gather.3.cloned.1.call-start = ((), (), s32[]{:S(2)}) async-start(), calls=%async_computation.1 | async-start | bytes 15482880 | tf_op jit(solution)/shard_map/all_gather | solution.py:32
  188.6 6.0 %copy-start.1 = (s32[800]{0:T(1024)S(1)}, s32[800]{0:T(1024)}, u32[]{:S(2)}) copy-start(s32[800]{0:T(1024)} %param.9) | copy-start | bytes 9604
  188.6 183.2 %all-to-all-start = ((f32[1,80,48,800]{3,2,0,1:T(8,128)}), f32[1,80,48,800]{3,2,0,1:T(8,128)}, u32[]{:S(2)}, u32[]{:S(2)}) async-start(f32[1,80,48,800]{3,2,0,1:T(8,128)} %copy.11), calls=%async_computation | async-start | bytes 27525120 | tf_op jit(solution)/shard_map/all_to_all | solution.py:33
  194.0 169.6 %all-gather.5.cloned.1.call-start = ((), (), s32[]{:S(2)}) async-start(), calls=%async_computation.2 | async-start | bytes 2506752 | tf_op jit(solution)/shard_map/all_gather | solution.py:31
  437.5 4.0 copy-start
Sparse Core Ops, SparseCore 0:
  16.4 157.8 all-gather.2
Sparse Core Ops, SparseCore 1:
  196.2 167.4 all-gather.4
where the time goes:
time: 486 us; the launch traced here: 483 us
  waiting for transfers between devices  322 us (66%)
  local copies, waits for them, and re-layouts  96.8 us (20%)
  matrix products  34.1 us (7%)
  between operations  15 us (3%)
  other arithmetic  9.62 us (2%)
  starting transfers between devices  5.47 us (1%)
    all_gather x1, waiting for transfers between devices, shards(): coupling = lax.all_gather(cycle_coupling, 'col', axis=2, tiled=True)  164 us
    all_gather x1, waiting for transfers between devices, shards(): across = lax.all_gather(stored, 'row', axis=2, tiled=True)  158 us
    dot_general x1, matrix products, contract_block(): jnp.einsum('rkc,kjcb->rjb', coupling, block, precision=lax.Precision.HIGH...  34.1 us
    all_to_all x2, local copies, waits for them, and re-layouts, shards(): lax.all_to_all(across, 'col', split_axis=1, concat_axis=2, tiled=True)  29.5 us
    gather x1, local copies, waits for them, and re-layouts, shards(): regrouped = jnp.take(regrouped, virtual_inverse, axis=3)  27.5 us
    all_gather x1, local copies, waits for them, and re-layouts, shards(): across = lax.all_gather(stored, 'row', axis=2, tiled=True)  14.3 us
  transfers between devices with their start and end apart: 3, of which 2 were waited for; matrix products, arithmetic and copies ran while one was open for 3% of the time, Pallas kernels for 0%

commit v1 on v0

v1 whole, which is shorter than its diff:
```python
import functools

import jax
import jax.numpy as jnp
from jax import lax
from jax.experimental import pallas as pl
from jax.experimental.pallas import tpu as pltpu
from jax.sharding import PartitionSpec as P

F32 = jnp.float32
BF16 = jnp.bfloat16
MESH = pl.DeviceIdType.MESH

LANES = 512
LAG_PERMUTE = -2
LAG_REGROUP = 0
LAG_FIRST = 1
LAG_SECOND = 2
LAG_MATMUL = 3

REGROUP, ACROSS, LOW, HIGH, FAR_LOW, FAR_HIGH, MIX_LOW, MIX_HIGH, MIXFAR_LOW, MIXFAR_HIGH = range(10)
EDGE_LOW, EDGE_HIGH, EDGE_FAR_LOW, EDGE_FAR_HIGH = range(10, 14)
KINDS = 14
W_ACROSS, W_ALONG, W_CORE = range(3)


def split(x):
    high = x.astype(BF16)
    return high, (x - high.astype(F32)).astype(BF16)


def kernel(
    chunks,
    occupied_ref,
    virtual_ref,
    amps_hbm,
    coupling_hbm,
    residual_ref,
    out_ref,
    amps,
    coupling_in,
    stored,
    picked,
    outgoing,
    incoming,
    panel,
    coupling_t,
    weights,
    factors,
    load_sem,
    send_sem,
    recv_sem,
    w_send_sem,
    w_recv_sem,
):
    step = pl.program_id(0)
    row = lax.axis_index("row")
    col = lax.axis_index("col")
    z, hi = row // 2, row % 2
    up, down, far = (z + 1) % 4, (z + 3) % 4, (z + 2) % 4
    across = (z * 2 + 1 - hi, col)
    above = (up * 2 + hi, col)
    below = (down * 2 + hi, col)
    width = LANES
    block = panel.shape[0] // 8
    blocks, virtual = picked.shape[0], picked.shape[2]
    cut = block // 6
    half = block // 2

    def lanes(chunk):
        return pl.ds(pl.multiple_of(chunk * width, width), width)

    def remote(src, dst, kind, chunk, where):
        pltpu.make_async_remote_copy(
            src_ref=src,
            dst_ref=dst,
            send_sem=send_sem.at[kind],
            recv_sem=recv_sem.at[chunk, kind],
            device_id=where,
            device_id_type=MESH,
        ).start()

    def rows(owner_z, owner_hi, first, count):
        start = (owner_z * 2 + owner_hi) * block + first
        return pl.ds(pl.multiple_of(start, 16), count)

    def push(owner_z, owner_hi, first, count, kind, chunk, where):
        ref = panel.at[rows(owner_z, owner_hi, first, count), lanes(chunk)]
        remote(ref, ref, kind, chunk, where)

    def arrived(kind, chunk, count):
        ref = panel.at[pl.ds(0, count), lanes(chunk)]
        pltpu.make_async_copy(ref, ref, recv_sem.at[chunk, kind]).wait()

    def pick(j):
        shape = (128, 480)
        r = lax.broadcasted_iota(jnp.int32, shape, 0)
        k = lax.broadcasted_iota(jnp.int32, shape, 1)
        wanted = jnp.where(r % 8 == k // 80, (r // 8) * blocks + j, -1)
        order = jnp.concatenate([occupied_ref[...]] * 6, axis=1)
        one_hot = (wanted == order).astype(F32).astype(BF16)
        for s in range(2):
            picked[j, pl.ds(128 * s, 128), :] = jnp.dot(
                one_hot, stored[s], preferred_element_type=F32
            ).astype(BF16)

    def permute(chunk, spanned=2):
        shape = (width, virtual)
        lane = lax.broadcasted_iota(jnp.int32, shape, 0) + chunk * width
        first = (chunk * width) // virtual
        total = jnp.zeros((256, width), F32)
        for n in range(spanned):
            j = jnp.minimum(first + n, blocks - 1)
            target = virtual_ref[...] + (first + n) * virtual
            one_hot = (lane == target).astype(F32).astype(BF16)
            total += lax.dot_general(
                picked[j], one_hot, (((1,), (1,)), ((), ())), preferred_element_type=F32
            )
        values = (total[:128] + total[128:]).reshape(16, 8, width)
        outgoing[:, :, lanes(chunk)] = values
        incoming[col, :, lanes(chunk)] = outgoing[col, :, lanes(chunk)]
        for d in range(1, 16):
            other = (col + d) % 16
            remote(
                outgoing.at[other, pl.ds(0, 6), lanes(chunk)],
                incoming.at[col, pl.ds(0, 6), lanes(chunk)],
                REGROUP,
                chunk,
                (row, other),
            )

    partners = [across, above, below]

    @pl.when(step == 0)
    def _():
        load_amps = pltpu.make_async_copy(amps_hbm, amps, load_sem.at[0])
        load_amps.start()
        load_coupling = pltpu.make_async_copy(coupling_hbm, coupling_in, load_sem.at[1])
        load_coupling.start()
        barrier = pltpu.get_barrier_semaphore()
        for where in partners:
            pl.semaphore_signal(barrier, inc=1, device_id=where, device_id_type=MESH)
        for d in range(1, 16):
            pl.semaphore_signal(barrier, inc=1, device_id=(row, (col + d) % 16), device_id_type=MESH)
        load_amps.wait()
        for i in range(6):
            high, low = split(amps[:, i * virtual : (i + 1) * virtual])
            stored[0, pl.ds(80 * i, 80), :] = high
            stored[1, pl.ds(80 * i, 80), :] = low
        pick(0)
        pl.semaphore_wait(barrier, 18)
        permute(0, pl.cdiv(width, virtual))
        load_coupling.wait()
        own = pl.ds(pl.multiple_of(col * 48, 16), 48)
        coupling_t[own, :] = coupling_in[...].reshape(768, 48).T
        pltpu.make_async_remote_copy(
            src_ref=coupling_t.at[own],
            dst_ref=coupling_t.at[own],
            send_sem=w_send_sem.at[W_ACROSS],
            recv_sem=w_recv_sem.at[W_ACROSS],
            device_id=(row, col // 4 * 4 + (col + 2) % 4),
            device_id_type=MESH,
        ).start()
        for j in range(1, blocks):
            pick(j)
        permute(1)

    def w_wait(sems, kind, count):
        ref = coupling_t.at[pl.ds(0, count)]
        pltpu.make_async_copy(ref, ref, sems.at[kind]).wait()

    def w_send(owner, kind, where):
        ref = coupling_t.at[pl.ds(pl.multiple_of(owner * 48, 16), 48)]
        pltpu.make_async_remote_copy(
            src_ref=ref,
            dst_ref=ref,
            send_sem=w_send_sem.at[kind],
            recv_sem=w_recv_sem.at[kind],
            device_id=where,
            device_id_type=MESH,
        ).start()

    chunk_r = step - LAG_REGROUP

    @pl.when((chunk_r >= 0) & (chunk_r < chunks))
    def _():
        ref = incoming.at[pl.ds(0, 15), pl.ds(0, 6), lanes(chunk_r)]
        pltpu.make_async_copy(ref, ref, recv_sem.at[chunk_r, REGROUP]).wait()
        pieces = [incoming[q, :, lanes(chunk_r)][:6] for q in range(16)]
        panel[rows(z, hi, 0, block), lanes(chunk_r)] = jnp.concatenate(pieces, axis=0)
        push(z, hi, 0, block, ACROSS, chunk_r, across)
        push(z, hi, 0, block, LOW, chunk_r, above)
        push(z, hi, 0, block, HIGH, chunk_r, below)

    chunk_f = step - LAG_FIRST

    @pl.when((chunk_f >= 0) & (chunk_f < chunks))
    def _():
        arrived(ACROSS, chunk_f, block)
        push(z, 1 - hi, cut, block - 2 * cut, MIX_LOW, chunk_f, above)
        push(z, 1 - hi, cut, block - 2 * cut, MIX_HIGH, chunk_f, below)
        arrived(LOW, chunk_f, block)
        push(down, hi, 0, half, FAR_LOW, chunk_f, above)
        push(down, hi, 0, cut, EDGE_LOW, chunk_f, across)
        push(down, hi, block - cut, cut, EDGE_LOW, chunk_f, across)
        arrived(HIGH, chunk_f, block)
        push(up, hi, half, half, FAR_HIGH, chunk_f, below)
        push(up, hi, 0, cut, EDGE_HIGH, chunk_f, across)
        push(up, hi, block - cut, cut, EDGE_HIGH, chunk_f, across)

    chunk_s = step - LAG_SECOND

    @pl.when((chunk_s >= 0) & (chunk_s < chunks))
    def _():
        arrived(MIX_LOW, chunk_s, block - 2 * cut)
        push(down, 1 - hi, cut, half - cut, MIXFAR_LOW, chunk_s, above)
        arrived(MIX_HIGH, chunk_s, block - 2 * cut)
        push(up, 1 - hi, half, half - cut, MIXFAR_HIGH, chunk_s, below)
        arrived(FAR_LOW, chunk_s, half)
        push(far, hi, 0, cut, EDGE_FAR_LOW, chunk_s, across)
        arrived(FAR_HIGH, chunk_s, half)
        push(far, hi, block - cut, cut, EDGE_FAR_HIGH, chunk_s, across)

    chunk_p = step - LAG_PERMUTE

    @pl.when(chunk_p < chunks)
    def _():
        permute(chunk_p)

    @pl.when(step == 1)
    def _():
        w_wait(w_recv_sem, W_ACROSS, 48)
        for d in range(1, 4):
            where = (row, (col + 4 * d) % 16)
            w_send(col, W_ALONG, where)
            w_send(col // 4 * 4 + (col + 2) % 4, W_ALONG, where)

    @pl.when(step == 2)
    def _():
        w_wait(w_recv_sem, W_ALONG, 48 * 6)
        where = (row, col // 2 * 2 + 1 - col % 2)
        for n in range(8):
            w_send(n * 2 + col % 2, W_CORE, where)

    @pl.when(step == LAG_MATMUL)
    def _():
        w_wait(w_recv_sem, W_CORE, 48 * 8)
        size = coupling_t.shape[0]
        high, low = split(coupling_t[...].T)
        weights[:, 0:size] = high
        weights[:, size : 2 * size] = low
        weights[:, 2 * size : 3 * size] = high

    chunk_m = step - LAG_MATMUL

    @pl.when(chunk_m >= 0)
    def _():
        arrived(EDGE_LOW, chunk_m, 2 * cut)
        arrived(EDGE_HIGH, chunk_m, 2 * cut)
        arrived(EDGE_FAR_LOW, chunk_m, cut)
        arrived(EDGE_FAR_HIGH, chunk_m, cut)
        arrived(MIXFAR_LOW, chunk_m, half - cut)
        arrived(MIXFAR_HIGH, chunk_m, half - cut)
        size = panel.shape[0]
        high, low = split(panel[:, lanes(chunk_m)])
        factors[0:size] = high
        factors[size : 2 * size] = high
        factors[2 * size : 3 * size] = low
        out_ref[...] = residual_ref[...] + jnp.dot(
            weights[...], factors[...], preferred_element_type=F32
        )

    @pl.when(step == pl.num_programs(0) - 1)
    def _():
        everything = pl.ds(0, chunks * width)
        ref = incoming.at[pl.ds(0, 15), pl.ds(0, 6), everything]
        pltpu.make_async_copy(ref, ref, send_sem.at[REGROUP]).wait()
        counts = {ACROSS: block, LOW: block, HIGH: block, FAR_LOW: half, FAR_HIGH: half}
        counts |= {MIX_LOW: block - 2 * cut, MIX_HIGH: block - 2 * cut, MIXFAR_LOW: half - cut}
        counts |= {MIXFAR_HIGH: half - cut, EDGE_LOW: 2 * cut, EDGE_HIGH: 2 * cut}
        counts |= {EDGE_FAR_LOW: cut, EDGE_FAR_HIGH: cut}
        for kind, count in counts.items():
            ref = panel.at[pl.ds(0, count), everything]
            pltpu.make_async_copy(ref, ref, send_sem.at[kind]).wait()
        w_wait(w_send_sem, W_ACROSS, 48)
        w_wait(w_send_sem, W_ALONG, 48 * 6)
        w_wait(w_send_sem, W_CORE, 48 * 8)


def shards(residual, cycle_coupling, pair_amps, occupied_order, virtual_order):
    occupied = occupied_order.shape[0]
    virtual = virtual_order.shape[0]
    local_rows, local_columns = residual.shape
    depth = local_rows
    chunks = pl.cdiv(local_columns, LANES)
    padded = chunks * LANES
    columns = local_columns // virtual
    steps = chunks + LAG_MATMUL

    def at(step):
        return 0, jnp.maximum(step - LAG_MATMUL, 0)

    def whole(shape):
        return pl.BlockSpec(shape, lambda step: (0, 0))

    anywhere = pl.BlockSpec(memory_space=pl.ANY)
    return pl.pallas_call(
        functools.partial(kernel, chunks),
        grid=(steps,),
        out_shape=jax.ShapeDtypeStruct(residual.shape, F32),
        in_specs=[
            whole((1, occupied)),
            whole((1, virtual)),
            anywhere,
            anywhere,
            pl.BlockSpec((local_rows, LANES), at),
        ],
        out_specs=pl.BlockSpec((local_rows, LANES), at),
        scratch_shapes=[
            pltpu.VMEM(pair_amps.shape, F32),
            pltpu.VMEM(cycle_coupling.shape, F32),
            pltpu.VMEM((2, 6 * occupied, virtual), BF16),
            pltpu.VMEM((columns, 256, virtual), BF16),
            pltpu.VMEM((16, 8, padded), F32),
            pltpu.VMEM((16, 8, padded), F32),
            pltpu.VMEM((depth, padded), F32),
            pltpu.VMEM((depth, local_rows), F32),
            pltpu.VMEM((local_rows, 3 * depth), BF16),
            pltpu.VMEM((3 * depth, LANES), BF16),
            pltpu.SemaphoreType.DMA((2,)),
            pltpu.SemaphoreType.DMA((KINDS,)),
            pltpu.SemaphoreType.DMA((chunks, KINDS)),
            pltpu.SemaphoreType.DMA((3,)),
            pltpu.SemaphoreType.DMA((3,)),
        ],
        compiler_params=pltpu.CompilerParams(
            collective_id=0, has_side_effects=True, vmem_limit_bytes=60 * 2**20
        ),
        cost_estimate=pl.CostEstimate(
            flops=6 * local_rows * depth * local_columns,
            bytes_accessed=8 * local_rows * local_columns,
            transcendentals=0,
        ),
    )(
        occupied_order.reshape(1, occupied),
        virtual_order.reshape(1, virtual),
        pair_amps,
        cycle_coupling,
        residual,
    )


def solution(mesh):
    in_specs = (P("row", "col"), P("row", None, "col"), P(None, ("row", "col")), P(), P())
    out_specs = P("row", "col")
    return jax.shard_map(shards, mesh=mesh, in_specs=in_specs, out_specs=out_specs, check_vma=False)
```

time: 486 us -> 138 us (0.28)
  waiting for transfers between devices: 322 us -> 0 us
  Pallas kernels: 0 us -> 109 us
  local copies, waits for them, and re-layouts: 96.8 us -> 28.3 us
  matrix products: 34.1 us -> 0 us
  between operations: 15 us -> 0.01 us
  other arithmetic: 9.62 us -> 0 us
  starting transfers between devices: 5.47 us -> 0 us
    all_gather x2 -> x0, waiting for transfers between devices: 322 us -> none  [the longest x1 164 us: shards(): coupling = lax.all_gather(cycle_coupling, 'col', axis=2, tiled=True)]
    pallas_call x0 -> x1, Pallas kernels: none -> 109 us  [shards(): pl.pallas_call(functools.partial(kernel, chunks), grid=(steps,), out_shap...]
    dot_general x1 -> x0, matrix products: 34.1 us -> none  [contract_block(): jnp.einsum('rkc,kjcb->rjb', coupling, block, precision=lax.Precision.HIGH...]
    gather x2 -> x0, local copies, waits for them, and re-layouts: 29.9 us -> none  [the longest x1 27.5 us: shards(): regrouped = jnp.take(regrouped, virtual_inverse, axis=3)]
    all_to_all x2 -> x0, local copies, waits for them, and re-layouts: 29.5 us -> none  [shards(): lax.all_to_all(across, 'col', split_axis=1, concat_axis=2, tiled=True)]
    unnamed x4 -> x2, local copies, waits for them, and re-layouts: 0.01 us -> 14.5 us
    all_gather x1 -> x0, local copies, waits for them, and re-layouts: 14.3 us -> none  [shards(): across = lax.all_gather(stored, 'row', axis=2, tiled=True)]
    pallas_call x0 -> x1, local copies, waits for them, and re-layouts: none -> 12.5 us  [shards(): pl.pallas_call(functools.partial(kernel, chunks), grid=(steps,), out_shap...]
  transfers between devices with their start and end apart: 3 -> 0, of which waited for: 2 -> 0; matrix products, arithmetic and copies ran while one was open for 3% -> 0% of each run, Pallas kernels for 0% -> 0%
where the time goes in v1:
time: 138 us; the launch traced here: 137 us
  Pallas kernels  109 us (79%)
  local copies, waits for them, and re-layouts  28.3 us (21%)
    pallas_call x1, Pallas kernels, shards(): pl.pallas_call(functools.partial(kernel, chunks), grid=(steps,), out_shap...  109 us
    unnamed x2, local copies, waits for them, and re-layouts  14.5 us
    pallas_call x1, local copies, waits for them, and re-layouts, shards(): pl.pallas_call(functools.partial(kernel, chunks), grid=(steps,), out_shap...  12.5 us

profile of v1, /device:TPU:24, one launch (start us, length us, event | category | flops | bytes accessed | tf_op | source)
XLA Modules:
  0.0 137.2 jit_solution(2068071805638089173)
XLA Ops:
  0.0 1.3 reshape.7.virtual_ref
  1.3 1.8 %copy.6.coupling_hbm = f32[768,1,48]{2,1,0:T(1,128)} copy(f32[768,1,48]{0,2,1:T(8,128)} %param.6) | data formatting | bytes 294912 | tf_op args[1]
  3.1 12.6 %copy.7.residual_ref = f32[768,4000]{1,0:T(8,128)} copy(f32[768,4000]{0,1:T(8,128)} %param.5) | data formatting | bytes 24576000 | tf_op args[0]
  15.8 108.9 %shard_map.55 = f32[768,4000]{1,0:T(8,128)} custom-call(s32[1,80]{1,0:T(1,128)} %bitcast.1, s32[1,800]{1,0:T(1,128)} %reshape.7.virtual_ref, f32[80,4800]{1,0:T(8,128)} %amps_hbm.1, f32[768,1,48]{2,1,0:T(1,128)} %copy.6.coupling_hbm, f32[768,4000]{1,0:T(8,128)} %copy.7.residual_ref), custom_call_target="tpu_custom_call" | custom-call | flops 14155776000 | bytes 24576000 | tf_op jit(solution)/shard_map/pallas_call | solution.py:307
  124.6 12.5 %copy.8 = f32[768,4000]{0,1:T(8,128)} copy(f32[768,4000]{1,0:T(8,128)} %shard_map.55) | data formatting | bytes 24576000 | tf_op jit(solution)/shard_map/pallas_call | solution.py:307

commit v2 on v1

--- a/solution.py
+++ b/solution.py
@@ -38,7 +38,6 @@
     residual_ref,
     out_ref,
     amps,
-    coupling_in,
     stored,
     picked,
     outgoing,
@@ -135,7 +134,8 @@
     def _():
         load_amps = pltpu.make_async_copy(amps_hbm, amps, load_sem.at[0])
         load_amps.start()
-        load_coupling = pltpu.make_async_copy(coupling_hbm, coupling_in, load_sem.at[1])
+        own = pl.ds(pl.multiple_of(col * 48, 16), 48)
+        load_coupling = pltpu.make_async_copy(coupling_hbm, coupling_t.at[own], load_sem.at[1])
         load_coupling.start()
         barrier = pltpu.get_barrier_semaphore()
         for where in partners:
@@ -151,8 +151,6 @@
         pl.semaphore_wait(barrier, 18)
         permute(0, pl.cdiv(width, virtual))
         load_coupling.wait()
-        own = pl.ds(pl.multiple_of(col * 48, 16), 48)
-        coupling_t[own, :] = coupling_in[...].reshape(768, 48).T
         pltpu.make_async_remote_copy(
             src_ref=coupling_t.at[own],
             dst_ref=coupling_t.at[own],
@@ -246,10 +244,10 @@
     def _():
         w_wait(w_recv_sem, W_CORE, 48 * 8)
         size = coupling_t.shape[0]
-        high, low = split(coupling_t[...].T)
-        weights[:, 0:size] = high
-        weights[:, size : 2 * size] = low
-        weights[:, 2 * size : 3 * size] = high
+        high, low = split(coupling_t[...])
+        weights[0:size] = high
+        weights[size : 2 * size] = low
+        weights[2 * size : 3 * size] = high
 
     chunk_m = step - LAG_MATMUL
 
@@ -262,12 +260,12 @@
         arrived(MIXFAR_LOW, chunk_m, half - cut)
         arrived(MIXFAR_HIGH, chunk_m, half - cut)
         size = panel.shape[0]
-        high, low = split(panel[:, lanes(chunk_m)])
-        factors[0:size] = high
-        factors[size : 2 * size] = high
-        factors[2 * size : 3 * size] = low
+        high, low = split(panel[:, lanes(chunk_m)].T)
+        factors[:, 0:size] = high
+        factors[:, size : 2 * size] = high
+        factors[:, 2 * size : 3 * size] = low
         out_ref[...] = residual_ref[...] + jnp.dot(
-            weights[...], factors[...], preferred_element_type=F32
+            factors[...], weights[...], preferred_element_type=F32
         )
 
     @pl.when(step == pl.num_programs(0) - 1)
@@ -291,6 +289,8 @@
     occupied = occupied_order.shape[0]
     virtual = virtual_order.shape[0]
     local_rows, local_columns = residual.shape
+    residual = residual.T
+    coupling = cycle_coupling.reshape(local_rows, cycle_coupling.shape[2]).T
     depth = local_rows
     chunks = pl.cdiv(local_columns, LANES)
     padded = chunks * LANES
@@ -298,7 +298,7 @@
     steps = chunks + LAG_MATMUL
 
     def at(step):
-        return 0, jnp.maximum(step - LAG_MATMUL, 0)
+        return jnp.maximum(step - LAG_MATMUL, 0), 0
 
     def whole(shape):
         return pl.BlockSpec(shape, lambda step: (0, 0))
@@ -313,20 +313,19 @@
             whole((1, virtual)),
             anywhere,
             anywhere,
-            pl.BlockSpec((local_rows, LANES), at),
+            pl.BlockSpec((LANES, local_rows), at),
         ],
-        out_specs=pl.BlockSpec((local_rows, LANES), at),
+        out_specs=pl.BlockSpec((LANES, local_rows), at),
         scratch_shapes=[
             pltpu.VMEM(pair_amps.shape, F32),
-            pltpu.VMEM(cycle_coupling.shape, F32),
             pltpu.VMEM((2, 6 * occupied, virtual), BF16),
             pltpu.VMEM((columns, 256, virtual), BF16),
             pltpu.VMEM((16, 8, padded), F32),
             pltpu.VMEM((16, 8, padded), F32),
             pltpu.VMEM((depth, padded), F32),
             pltpu.VMEM((depth, local_rows), F32),
-            pltpu.VMEM((local_rows, 3 * depth), BF16),
-            pltpu.VMEM((3 * depth, LANES), BF16),
+            pltpu.VMEM((3 * depth, local_rows), BF16),
+            pltpu.VMEM((LANES, 3 * depth), BF16),
             pltpu.SemaphoreType.DMA((2,)),
             pltpu.SemaphoreType.DMA((KINDS,)),
             pltpu.SemaphoreType.DMA((chunks, KINDS)),
@@ -345,9 +344,9 @@
         occupied_order.reshape(1, occupied),
         virtual_order.reshape(1, virtual),
         pair_amps,
-        cycle_coupling,
+        coupling,
         residual,
-    )
+    ).T
 
 
 def solution(mesh):

time: 138 us -> 121 us (0.88)
  local copies, waits for them, and re-layouts: 28.3 us -> 11.2 us
    pallas_call x1 -> x0, local copies, waits for them, and re-layouts: 12.5 us -> none  [shards(): pl.pallas_call(functools.partial(kernel, chunks), grid=(steps,), out_shap...]
    unnamed x2 -> x1, local copies, waits for them, and re-layouts: 14.5 us -> 9.96 us
where the time goes in v2:
time: 121 us; the launch traced here: 120 us
  Pallas kernels  109 us (90%)
  local copies, waits for them, and re-layouts  11.2 us (9%)
    pallas_call x1, Pallas kernels, shards(): pl.pallas_call(functools.partial(kernel, chunks), grid=(steps,), out_shap...  109 us
    unnamed x1, local copies, waits for them, and re-layouts  9.96 us

profile of v2, /device:TPU:24, one launch (start us, length us, event | category | flops | bytes accessed | tf_op | source)
XLA Modules:
  0.0 120.4 jit_solution(2547451618796490710)
XLA Ops:
  0.0 1.3 %reshape.10.virtual_ref = s32[1,800]{1,0:T(1,128)} reshape(s32[800]{0:T(1024)} %param.9) | data formatting | bytes 6400 | tf_op jit(solution)/shard_map/reshape | solution.py:345
  1.3 109.1 %shard_map.55 = f32[4000,768]{1,0:T(8,128)} custom-call(s32[1,80]{1,0:T(1,128)} %bitcast.9, s32[1,800]{1,0:T(1,128)} %reshape.10.virtual_ref, f32[80,4800]{1,0:T(8,128)} %amps_hbm.1, f32[48,768]{1,0:T(8,128)} %bitcast.8, f32[4000,768]{1,0:T(8,128)} %bitcast.7), custom_call_target="tpu_custom_call" | custom-call | flops 14155776000 | bytes 24576000 | tf_op jit(solution)/shard_map/pallas_call | solution.py:307
  110.4 10.0 %copy.7 = f32[768,4000]{0,1:T(8,128)} copy(f32[768,4000]{0,1:T(8,128)} %bitcast.6) | data formatting | bytes 24576000

commit v3 on v2

--- a/solution.py
+++ b/solution.py
@@ -12,15 +12,15 @@
 MESH = pl.DeviceIdType.MESH
 
 LANES = 512
-LAG_PERMUTE = -2
 LAG_REGROUP = 0
 LAG_FIRST = 1
 LAG_SECOND = 2
 LAG_MATMUL = 3
 
 REGROUP, ACROSS, LOW, HIGH, FAR_LOW, FAR_HIGH, MIX_LOW, MIX_HIGH, MIXFAR_LOW, MIXFAR_HIGH = range(10)
-EDGE_LOW, EDGE_HIGH, EDGE_FAR_LOW, EDGE_FAR_HIGH = range(10, 14)
-KINDS = 14
+EDGE_LOW, EDGE_HIGH, EDGE_FAR = range(10, 13)
+KINDS = 13
+GROUPS = {first: 1 for first in range(8)}
 W_ACROSS, W_ALONG, W_CORE = range(3)
 
 
@@ -36,7 +36,7 @@
     amps_hbm,
     coupling_hbm,
     residual_ref,
-    out_ref,
+    out_hbm,
     amps,
     stored,
     picked,
@@ -46,7 +46,9 @@
     coupling_t,
     weights,
     factors,
+    results,
     load_sem,
+    store_sem,
     send_sem,
     recv_sem,
     w_send_sem,
@@ -63,8 +65,10 @@
     width = LANES
     block = panel.shape[0] // 8
     blocks, virtual = picked.shape[0], picked.shape[2]
-    cut = block // 6
+    cut = block // 3
+    mixed = block - cut
     half = block // 2
+    middle = cut + mixed // 2
 
     def lanes(chunk):
         return pl.ds(pl.multiple_of(chunk * width, width), width)
@@ -110,7 +114,7 @@
         total = jnp.zeros((256, width), F32)
         for n in range(spanned):
             j = jnp.minimum(first + n, blocks - 1)
-            target = virtual_ref[...] + (first + n) * virtual
+            target = virtual_ref[...].reshape(1, virtual) + (first + n) * virtual
             one_hot = (lane == target).astype(F32).astype(BF16)
             total += lax.dot_general(
                 picked[j], one_hot, (((1,), (1,)), ((), ())), preferred_element_type=F32
@@ -118,13 +122,18 @@
         values = (total[:128] + total[128:]).reshape(16, 8, width)
         outgoing[:, :, lanes(chunk)] = values
         incoming[col, :, lanes(chunk)] = outgoing[col, :, lanes(chunk)]
+
+    def group_lanes(first):
+        return pl.ds(first * width, GROUPS[first] * width)
+
+    def regroup(first):
         for d in range(1, 16):
             other = (col + d) % 16
             remote(
-                outgoing.at[other, pl.ds(0, 6), lanes(chunk)],
-                incoming.at[col, pl.ds(0, 6), lanes(chunk)],
+                outgoing.at[other, pl.ds(0, 6), group_lanes(first)],
+                incoming.at[col, pl.ds(0, 6), group_lanes(first)],
                 REGROUP,
-                chunk,
+                first,
                 (row, other),
             )
 
@@ -148,8 +157,9 @@
             stored[0, pl.ds(80 * i, 80), :] = high
             stored[1, pl.ds(80 * i, 80), :] = low
         pick(0)
+        permute(0, pl.cdiv(width, virtual))
         pl.semaphore_wait(barrier, 18)
-        permute(0, pl.cdiv(width, virtual))
+        regroup(0)
         load_coupling.wait()
         pltpu.make_async_remote_copy(
             src_ref=coupling_t.at[own],
@@ -159,9 +169,9 @@
             device_id=(row, col // 4 * 4 + (col + 2) % 4),
             device_id_type=MESH,
         ).start()
-        for j in range(1, blocks):
-            pick(j)
+        pick(1)
         permute(1)
+        regroup(1)
 
     def w_wait(sems, kind, count):
         ref = coupling_t.at[pl.ds(0, count)]
@@ -182,8 +192,13 @@
 
     @pl.when((chunk_r >= 0) & (chunk_r < chunks))
     def _():
-        ref = incoming.at[pl.ds(0, 15), pl.ds(0, 6), lanes(chunk_r)]
-        pltpu.make_async_copy(ref, ref, recv_sem.at[chunk_r, REGROUP]).wait()
+        for first in GROUPS:
+
+            @pl.when(chunk_r == first)
+            def _(first=first):
+                ref = incoming.at[pl.ds(0, 15), pl.ds(0, 6), group_lanes(first)]
+                pltpu.make_async_copy(ref, ref, recv_sem.at[first, REGROUP]).wait()
+
         pieces = [incoming[q, :, lanes(chunk_r)][:6] for q in range(16)]
         panel[rows(z, hi, 0, block), lanes(chunk_r)] = jnp.concatenate(pieces, axis=0)
         push(z, hi, 0, block, ACROSS, chunk_r, across)
@@ -195,35 +210,58 @@
     @pl.when((chunk_f >= 0) & (chunk_f < chunks))
     def _():
         arrived(ACROSS, chunk_f, block)
-        push(z, 1 - hi, cut, block - 2 * cut, MIX_LOW, chunk_f, above)
-        push(z, 1 - hi, cut, block - 2 * cut, MIX_HIGH, chunk_f, below)
+        push(z, 1 - hi, cut, mixed, MIX_LOW, chunk_f, above)
+        push(z, 1 - hi, cut, mixed, MIX_HIGH, chunk_f, below)
         arrived(LOW, chunk_f, block)
         push(down, hi, 0, half, FAR_LOW, chunk_f, above)
         push(down, hi, 0, cut, EDGE_LOW, chunk_f, across)
-        push(down, hi, block - cut, cut, EDGE_LOW, chunk_f, across)
         arrived(HIGH, chunk_f, block)
         push(up, hi, half, half, FAR_HIGH, chunk_f, below)
         push(up, hi, 0, cut, EDGE_HIGH, chunk_f, across)
-        push(up, hi, block - cut, cut, EDGE_HIGH, chunk_f, across)
 
     chunk_s = step - LAG_SECOND
 
     @pl.when((chunk_s >= 0) & (chunk_s < chunks))
     def _():
-        arrived(MIX_LOW, chunk_s, block - 2 * cut)
-        push(down, 1 - hi, cut, half - cut, MIXFAR_LOW, chunk_s, above)
-        arrived(MIX_HIGH, chunk_s, block - 2 * cut)
-        push(up, 1 - hi, half, half - cut, MIXFAR_HIGH, chunk_s, below)
+        arrived(MIX_LOW, chunk_s, mixed)
+        push(down, 1 - hi, cut, mixed // 2, MIXFAR_LOW, chunk_s, above)
+        arrived(MIX_HIGH, chunk_s, mixed)
+        push(up, 1 - hi, middle, mixed // 2, MIXFAR_HIGH, chunk_s, below)
         arrived(FAR_LOW, chunk_s, half)
-        push(far, hi, 0, cut, EDGE_FAR_LOW, chunk_s, across)
-        arrived(FAR_HIGH, chunk_s, half)
-        push(far, hi, block - cut, cut, EDGE_FAR_HIGH, chunk_s, across)
-
-    chunk_p = step - LAG_PERMUTE
-
-    @pl.when(chunk_p < chunks)
-    def _():
-        permute(chunk_p)
+        push(far, hi, 0, cut, EDGE_FAR, chunk_s, across)
+
+    @pl.when(step == 0)
+    def _():
+        pick(2)
+        permute(2)
+        regroup(2)
+
+    @pl.when(step == 1)
+    def _():
+        pick(3)
+        permute(3)
+        regroup(3)
+        pick(4)
+
+    @pl.when(step == 2)
+    def _():
+        permute(4)
+        regroup(4)
+
+    @pl.when(step == 3)
+    def _():
+        permute(5)
+        regroup(5)
+
+    @pl.when(step == 4)
+    def _():
+        permute(6)
+        regroup(6)
+
+    @pl.when(step == 5)
+    def _():
+        permute(7)
+        regroup(7)
 
     @pl.when(step == 1)
     def _():
@@ -250,33 +288,57 @@
         weights[2 * size : 3 * size] = high
 
     chunk_m = step - LAG_MATMUL
+    last = out_hbm.shape[0] - (chunks - 1) * width
+
+    def store(chunk, count):
+        start = pl.multiple_of(chunk * width, width)
+        return pltpu.make_async_copy(
+            results.at[chunk % 2, pl.ds(0, count)],
+            out_hbm.at[pl.ds(start, count)],
+            store_sem.at[chunk % 2],
+        )
 
     @pl.when(chunk_m >= 0)
     def _():
-        arrived(EDGE_LOW, chunk_m, 2 * cut)
-        arrived(EDGE_HIGH, chunk_m, 2 * cut)
-        arrived(EDGE_FAR_LOW, chunk_m, cut)
-        arrived(EDGE_FAR_HIGH, chunk_m, cut)
-        arrived(MIXFAR_LOW, chunk_m, half - cut)
-        arrived(MIXFAR_HIGH, chunk_m, half - cut)
+        arrived(FAR_HIGH, chunk_m, half)
+        arrived(EDGE_LOW, chunk_m, cut)
+        arrived(EDGE_HIGH, chunk_m, cut)
+        arrived(EDGE_FAR, chunk_m, cut)
+        arrived(MIXFAR_LOW, chunk_m, mixed // 2)
+        arrived(MIXFAR_HIGH, chunk_m, mixed // 2)
         size = panel.shape[0]
         high, low = split(panel[:, lanes(chunk_m)].T)
         factors[:, 0:size] = high
         factors[:, size : 2 * size] = high
         factors[:, 2 * size : 3 * size] = low
-        out_ref[...] = residual_ref[...] + jnp.dot(
+        slot = chunk_m % 2
+
+        @pl.when(chunk_m >= 2)
+        def _():
+            store(chunk_m - 2, width).wait()
+
+        results[slot] = residual_ref[...] + jnp.dot(
             factors[...], weights[...], preferred_element_type=F32
         )
 
+        @pl.when(chunk_m < chunks - 1)
+        def _():
+            store(chunk_m, width).start()
+
+        @pl.when(chunk_m == chunks - 1)
+        def _():
+            store(chunks - 1, last).start()
+
     @pl.when(step == pl.num_programs(0) - 1)
     def _():
+        store(chunks - 2, width).wait()
+        store(chunks - 1, last).wait()
         everything = pl.ds(0, chunks * width)
         ref = incoming.at[pl.ds(0, 15), pl.ds(0, 6), everything]
         pltpu.make_async_copy(ref, ref, send_sem.at[REGROUP]).wait()
         counts = {ACROSS: block, LOW: block, HIGH: block, FAR_LOW: half, FAR_HIGH: half}
-        counts |= {MIX_LOW: block - 2 * cut, MIX_HIGH: block - 2 * cut, MIXFAR_LOW: half - cut}
-        counts |= {MIXFAR_HIGH: half - cut, EDGE_LOW: 2 * cut, EDGE_HIGH: 2 * cut}
-        counts |= {EDGE_FAR_LOW: cut, EDGE_FAR_HIGH: cut}
+        counts |= {MIX_LOW: mixed, MIX_HIGH: mixed, EDGE_LOW: cut, EDGE_HIGH: cut, EDGE_FAR: cut}
+        counts |= {MIXFAR_LOW: mixed // 2, MIXFAR_HIGH: mixed // 2}
         for kind, count in counts.items():
             ref = panel.at[pl.ds(0, count), everything]
             pltpu.make_async_copy(ref, ref, send_sem.at[kind]).wait()
@@ -307,15 +369,15 @@
     return pl.pallas_call(
         functools.partial(kernel, chunks),
         grid=(steps,),
-        out_shape=jax.ShapeDtypeStruct(residual.shape, F32),
+        out_shape=pltpu.VMEM(residual.shape, F32),
         in_specs=[
             whole((1, occupied)),
-            whole((1, virtual)),
+            pl.BlockSpec((virtual,), lambda step: (0,)),
             anywhere,
             anywhere,
             pl.BlockSpec((LANES, local_rows), at),
         ],
-        out_specs=pl.BlockSpec((LANES, local_rows), at),
+        out_specs=anywhere,
         scratch_shapes=[
             pltpu.VMEM(pair_amps.shape, F32),
             pltpu.VMEM((2, 6 * occupied, virtual), BF16),
@@ -326,6 +388,8 @@
             pltpu.VMEM((depth, local_rows), F32),
             pltpu.VMEM((3 * depth, local_rows), BF16),
             pltpu.VMEM((LANES, 3 * depth), BF16),
+            pltpu.VMEM((2, LANES, local_rows), F32),
+            pltpu.SemaphoreType.DMA((2,)),
             pltpu.SemaphoreType.DMA((2,)),
             pltpu.SemaphoreType.DMA((KINDS,)),
             pltpu.SemaphoreType.DMA((chunks, KINDS)),
@@ -333,7 +397,7 @@
             pltpu.SemaphoreType.DMA((3,)),
         ],
         compiler_params=pltpu.CompilerParams(
-            collective_id=0, has_side_effects=True, vmem_limit_bytes=60 * 2**20
+            collective_id=0, has_side_effects=True, vmem_limit_bytes=48 * 2**20
         ),
         cost_estimate=pl.CostEstimate(
             flops=6 * local_rows * depth * local_columns,
@@ -342,7 +406,7 @@
         ),
     )(
         occupied_order.reshape(1, occupied),
-        virtual_order.reshape(1, virtual),
+        virtual_order,
         pair_amps,
         coupling,
         residual,

time: 121 us -> 114 us (0.942)
  local copies, waits for them, and re-layouts: 11.2 us -> 4.68 us
    unnamed x1, local copies, waits for them, and re-layouts: 9.96 us -> 4.68 us
    reshape x1 -> x0, local copies, waits for them, and re-layouts: 1.27 us -> none  [shards(): virtual_order.reshape(1, virtual)]
where the time goes in v3:
time: 114 us
  Pallas kernels  109 us (96%)
  local copies, waits for them, and re-layouts  4.68 us (4%)
    pallas_call x1, Pallas kernels, shards(): pl.pallas_call(functools.partial(kernel, chunks), grid=(steps,), out_shap...  109 us
    unnamed x1, local copies, waits for them, and re-layouts  4.68 us

profile of v3, /device:TPU:24, one launch (start us, length us, event | category | flops | bytes accessed | tf_op | source)
XLA Modules:
  0.0 113.7 jit_solution(2281359829423937587)
XLA Ops:
  0.0 109.0 %shard_map.55 = f32[4000,768]{1,0:T(8,128)S(1)} custom-call(s32[1,80]{1,0:T(1,128)} %bitcast.9, s32[800]{0:T(1024)} %virtual_ref.1, f32[80,4800]{1,0:T(8,128)} %amps_hbm.1, f32[48,768]{1,0:T(8,128)} %bitcast.8, f32[4000,768]{1,0:T(8,128)} %bitcast.7), custom_call_target="tpu_custom_call" | custom-call | flops 14155776000 | bytes 24576000 | tf_op jit(solution)/shard_map/pallas_call | solution.py:369
  109.0 4.7 %copy.7 = f32[768,4000]{0,1:T(8,128)} copy(f32[768,4000]{0,1:T(8,128)S(1)} %bitcast.6) | data formatting | bytes 24576000

commit v4 on v3

--- a/solution.py
+++ b/solution.py
@@ -38,6 +38,8 @@
     residual_ref,
     out_hbm,
     amps,
+    distance,
+    column,
     stored,
     picked,
     outgoing,
@@ -96,28 +98,25 @@
         pltpu.make_async_copy(ref, ref, recv_sem.at[chunk, kind]).wait()
 
     def pick(j):
-        shape = (128, 480)
-        r = lax.broadcasted_iota(jnp.int32, shape, 0)
-        k = lax.broadcasted_iota(jnp.int32, shape, 1)
-        wanted = jnp.where(r % 8 == k // 80, (r // 8) * blocks + j, -1)
-        order = jnp.concatenate([occupied_ref[...]] * 6, axis=1)
-        one_hot = (wanted == order).astype(F32).astype(BF16)
+        one_hot = (distance[...] == j).astype(F32).astype(BF16)
         for s in range(2):
             picked[j, pl.ds(128 * s, 128), :] = jnp.dot(
                 one_hot, stored[s], preferred_element_type=F32
             ).astype(BF16)
 
     def permute(chunk, spanned=2):
-        shape = (width, virtual)
-        lane = lax.broadcasted_iota(jnp.int32, shape, 0) + chunk * width
+        lane = lax.broadcasted_iota(jnp.int32, (virtual, 128), 1)
         first = (chunk * width) // virtual
         total = jnp.zeros((256, width), F32)
         for n in range(spanned):
             j = jnp.minimum(first + n, blocks - 1)
-            target = virtual_ref[...].reshape(1, virtual) + (first + n) * virtual
-            one_hot = (lane == target).astype(F32).astype(BF16)
-            total += lax.dot_general(
-                picked[j], one_hot, (((1,), (1,)), ((), ())), preferred_element_type=F32
+            gap = lane - column[...]
+            shift = (first + n) * virtual - chunk * width
+            parts = [
+                (gap == shift - start).astype(F32).astype(BF16) for start in range(0, width, 128)
+            ]
+            total += jnp.dot(
+                picked[j], jnp.concatenate(parts, axis=1), preferred_element_type=F32
             )
         values = (total[:128] + total[128:]).reshape(16, 8, width)
         outgoing[:, :, lanes(chunk)] = values
@@ -137,6 +136,21 @@
                 (row, other),
             )
 
+    def w_wait(sems, kind, count):
+        ref = coupling_t.at[pl.ds(0, count)]
+        pltpu.make_async_copy(ref, ref, sems.at[kind]).wait()
+
+    def w_send(owner, kind, where):
+        ref = coupling_t.at[pl.ds(pl.multiple_of(owner * 48, 16), 48)]
+        pltpu.make_async_remote_copy(
+            src_ref=ref,
+            dst_ref=ref,
+            send_sem=w_send_sem.at[kind],
+            recv_sem=w_recv_sem.at[kind],
+            device_id=where,
+            device_id_type=MESH,
+        ).start()
+
     partners = [across, above, below]
 
     @pl.when(step == 0)
@@ -151,6 +165,11 @@
             pl.semaphore_signal(barrier, inc=1, device_id=where, device_id_type=MESH)
         for d in range(1, 16):
             pl.semaphore_signal(barrier, inc=1, device_id=(row, (col + d) % 16), device_id_type=MESH)
+        r = lax.broadcasted_iota(jnp.int32, (128, 480), 0)
+        k = lax.broadcasted_iota(jnp.int32, (128, 480), 1)
+        order = jnp.concatenate([occupied_ref[...]] * 6, axis=1)
+        distance[...] = jnp.where(r % 8 == k // 80, order - (r // 8) * blocks, -1)
+        column[...] = jnp.broadcast_to(virtual_ref[...].reshape(1, virtual), (128, virtual)).T
         load_amps.wait()
         for i in range(6):
             high, low = split(amps[:, i * virtual : (i + 1) * virtual])
@@ -161,32 +180,12 @@
         pl.semaphore_wait(barrier, 18)
         regroup(0)
         load_coupling.wait()
-        pltpu.make_async_remote_copy(
-            src_ref=coupling_t.at[own],
-            dst_ref=coupling_t.at[own],
-            send_sem=w_send_sem.at[W_ACROSS],
-            recv_sem=w_recv_sem.at[W_ACROSS],
-            device_id=(row, col // 4 * 4 + (col + 2) % 4),
-            device_id_type=MESH,
-        ).start()
+        w_send(col, W_ACROSS, (row, col // 4 * 4 + (col + 2) % 4))
         pick(1)
         permute(1)
         regroup(1)
-
-    def w_wait(sems, kind, count):
-        ref = coupling_t.at[pl.ds(0, count)]
-        pltpu.make_async_copy(ref, ref, sems.at[kind]).wait()
-
-    def w_send(owner, kind, where):
-        ref = coupling_t.at[pl.ds(pl.multiple_of(owner * 48, 16), 48)]
-        pltpu.make_async_remote_copy(
-            src_ref=ref,
-            dst_ref=ref,
-            send_sem=w_send_sem.at[kind],
-            recv_sem=w_recv_sem.at[kind],
-            device_id=where,
-            device_id_type=MESH,
-        ).start()
+        for d in range(1, 4):
+            w_send(col, W_ALONG, (row, (col + 4 * d) % 16))
 
     chunk_r = step - LAG_REGROUP
 
@@ -263,15 +262,13 @@
         permute(7)
         regroup(7)
 
-    @pl.when(step == 1)
+    @pl.when(step == 0)
     def _():
         w_wait(w_recv_sem, W_ACROSS, 48)
         for d in range(1, 4):
-            where = (row, (col + 4 * d) % 16)
-            w_send(col, W_ALONG, where)
-            w_send(col // 4 * 4 + (col + 2) % 4, W_ALONG, where)
-
-    @pl.when(step == 2)
+            w_send(col // 4 * 4 + (col + 2) % 4, W_ALONG, (row, (col + 4 * d) % 16))
+
+    @pl.when(step == LAG_MATMUL)
     def _():
         w_wait(w_recv_sem, W_ALONG, 48 * 6)
         where = (row, col // 2 * 2 + 1 - col % 2)
@@ -380,6 +377,8 @@
         out_specs=anywhere,
         scratch_shapes=[
             pltpu.VMEM(pair_amps.shape, F32),
+            pltpu.VMEM((128, 6 * occupied), jnp.int32),
+            pltpu.VMEM((virtual, 128), jnp.int32),
             pltpu.VMEM((2, 6 * occupied, virtual), BF16),
             pltpu.VMEM((columns, 256, virtual), BF16),
             pltpu.VMEM((16, 8, padded), F32),

time: 114 us -> 112 us (0.982)
  Pallas kernels: 109 us -> 106 us
    pallas_call x1, Pallas kernels: 109 us -> 106 us  [shards(): pl.pallas_call(functools.partial(kernel, chunks), grid=(steps,), out_shap...]
where the time goes in v4:
time: 112 us; the launch traced here: 111 us
  Pallas kernels  106 us (95%)
  local copies, waits for them, and re-layouts  4.68 us (4%)
    pallas_call x1, Pallas kernels, shards(): pl.pallas_call(functools.partial(kernel, chunks), grid=(steps,), out_shap...  106 us
    unnamed x1, local copies, waits for them, and re-layouts  4.68 us

profile of v4, /device:TPU:24, one launch (start us, length us, event | category | flops | bytes accessed | tf_op | source)
XLA Modules:
  0.0 110.8 jit_solution(4076253436378396517)
XLA Ops:
  0.0 106.1 %shard_map.55 = f32[4000,768]{1,0:T(8,128)S(1)} custom-call(s32[1,80]{1,0:T(1,128)} %bitcast.9, s32[800]{0:T(1024)} %virtual_ref.1, f32[80,4800]{1,0:T(8,128)} %amps_hbm.1, f32[48,768]{1,0:T(8,128)} %bitcast.8, f32[4000,768]{1,0:T(8,128)} %bitcast.7), custom_call_target="tpu_custom_call" | custom-call | flops 14155776000 | bytes 24576000 | tf_op jit(solution)/shard_map/pallas_call | solution.py:366
  106.1 4.7 %copy.7 = f32[768,4000]{0,1:T(8,128)} copy(f32[768,4000]{0,1:T(8,128)S(1)} %bitcast.6) | data formatting | bytes 24576000

commit v5 on v4

--- a/solution.py
+++ b/solution.py
@@ -13,6 +13,8 @@
 
 LANES = 512
 LAG_REGROUP = 0
+CUT_EVEN = 32
+CUT_ODD = 40
 LAG_FIRST = 1
 LAG_SECOND = 2
 LAG_MATMUL = 3
@@ -61,16 +63,20 @@
     col = lax.axis_index("col")
     z, hi = row // 2, row % 2
     up, down, far = (z + 1) % 4, (z + 3) % 4, (z + 2) % 4
+    lo = col // 2 % 2
+
+    def swapped_from(parity):
+        return (lo + parity) % 2
+
     across = (z * 2 + 1 - hi, col)
     above = (up * 2 + hi, col)
     below = (down * 2 + hi, col)
     width = LANES
     block = panel.shape[0] // 8
     blocks, virtual = picked.shape[0], picked.shape[2]
-    cut = block // 3
-    mixed = block - cut
     half = block // 2
-    middle = cut + mixed // 2
+    cuts = (CUT_EVEN, CUT_ODD)
+    lows = tuple(pl.cdiv(block - cut, 16) * 8 for cut in cuts)
 
     def lanes(chunk):
         return pl.ds(pl.multiple_of(chunk * width, width), width)
@@ -87,7 +93,7 @@
 
     def rows(owner_z, owner_hi, first, count):
         start = (owner_z * 2 + owner_hi) * block + first
-        return pl.ds(pl.multiple_of(start, 16), count)
+        return pl.ds(pl.multiple_of(start, 8), count)
 
     def push(owner_z, owner_hi, first, count, kind, chunk, where):
         ref = panel.at[rows(owner_z, owner_hi, first, count), lanes(chunk)]
@@ -128,12 +134,13 @@
     def regroup(first):
         for d in range(1, 16):
             other = (col + d) % 16
+            crossed = ((other // 2 % 2 != lo) & (swapped_from(first % 2) == 1)).astype(jnp.int32)
             remote(
                 outgoing.at[other, pl.ds(0, 6), group_lanes(first)],
                 incoming.at[col, pl.ds(0, 6), group_lanes(first)],
                 REGROUP,
                 first,
-                (row, other),
+                (z * 2 + (hi + crossed) % 2, other),
             )
 
     def w_wait(sems, kind, count):
@@ -165,6 +172,9 @@
             pl.semaphore_signal(barrier, inc=1, device_id=where, device_id_type=MESH)
         for d in range(1, 16):
             pl.semaphore_signal(barrier, inc=1, device_id=(row, (col + d) % 16), device_id_type=MESH)
+        for n in range(8):
+            other = n // 2 * 4 + (1 - lo) * 2 + n % 2
+            pl.semaphore_signal(barrier, inc=1, device_id=(across[0], other), device_id_type=MESH)
         r = lax.broadcasted_iota(jnp.int32, (128, 480), 0)
         k = lax.broadcasted_iota(jnp.int32, (128, 480), 1)
         order = jnp.concatenate([occupied_ref[...]] * 6, axis=1)
@@ -177,7 +187,7 @@
             stored[1, pl.ds(80 * i, 80), :] = low
         pick(0)
         permute(0, pl.cdiv(width, virtual))
-        pl.semaphore_wait(barrier, 18)
+        pl.semaphore_wait(barrier, 26)
         regroup(0)
         load_coupling.wait()
         w_send(col, W_ACROSS, (row, col // 4 * 4 + (col + 2) % 4))
@@ -204,30 +214,42 @@
         push(z, hi, 0, block, LOW, chunk_r, above)
         push(z, hi, 0, block, HIGH, chunk_r, below)
 
-    chunk_f = step - LAG_FIRST
-
-    @pl.when((chunk_f >= 0) & (chunk_f < chunks))
-    def _():
-        arrived(ACROSS, chunk_f, block)
-        push(z, 1 - hi, cut, mixed, MIX_LOW, chunk_f, above)
-        push(z, 1 - hi, cut, mixed, MIX_HIGH, chunk_f, below)
-        arrived(LOW, chunk_f, block)
-        push(down, hi, 0, half, FAR_LOW, chunk_f, above)
-        push(down, hi, 0, cut, EDGE_LOW, chunk_f, across)
-        arrived(HIGH, chunk_f, block)
-        push(up, hi, half, half, FAR_HIGH, chunk_f, below)
-        push(up, hi, 0, cut, EDGE_HIGH, chunk_f, across)
-
-    chunk_s = step - LAG_SECOND
-
-    @pl.when((chunk_s >= 0) & (chunk_s < chunks))
-    def _():
-        arrived(MIX_LOW, chunk_s, mixed)
-        push(down, 1 - hi, cut, mixed // 2, MIXFAR_LOW, chunk_s, above)
-        arrived(MIX_HIGH, chunk_s, mixed)
-        push(up, 1 - hi, middle, mixed // 2, MIXFAR_HIGH, chunk_s, below)
-        arrived(FAR_LOW, chunk_s, half)
-        push(far, hi, 0, cut, EDGE_FAR, chunk_s, across)
+    def first_stage(chunk, cut, low):
+        arrived(ACROSS, chunk, block)
+        push(z, 1 - hi, cut, block - cut, MIX_LOW, chunk, above)
+        push(z, 1 - hi, cut, block - cut, MIX_HIGH, chunk, below)
+        arrived(LOW, chunk, block)
+        push(down, hi, 0, half, FAR_LOW, chunk, above)
+        push(down, hi, 0, cut, EDGE_LOW, chunk, across)
+        arrived(HIGH, chunk, block)
+        push(up, hi, half, half, FAR_HIGH, chunk, below)
+        push(up, hi, 0, cut, EDGE_HIGH, chunk, across)
+
+    def second_stage(chunk, cut, low):
+        arrived(MIX_LOW, chunk, block - cut)
+        push(down, 1 - hi, cut, low, MIXFAR_LOW, chunk, above)
+        arrived(MIX_HIGH, chunk, block - cut)
+        push(up, 1 - hi, cut + low, block - cut - low, MIXFAR_HIGH, chunk, below)
+        arrived(FAR_LOW, chunk, half)
+        push(far, hi, 0, cut, EDGE_FAR, chunk, across)
+
+    def last_stage(chunk, cut, low):
+        arrived(FAR_HIGH, chunk, half)
+        arrived(EDGE_LOW, chunk, cut)
+        arrived(EDGE_HIGH, chunk, cut)
+        arrived(EDGE_FAR, chunk, cut)
+        arrived(MIXFAR_LOW, chunk, low)
+        arrived(MIXFAR_HIGH, chunk, block - cut - low)
+
+    def by_parity(stage, chunk):
+        for parity in range(2):
+
+            @pl.when((chunk >= 0) & (chunk < chunks) & (chunk % 2 == parity))
+            def _(parity=parity):
+                stage(chunk, cuts[parity], lows[parity])
+
+    by_parity(first_stage, step - LAG_FIRST)
+    by_parity(second_stage, step - LAG_SECOND)
 
     @pl.when(step == 0)
     def _():
@@ -279,10 +301,17 @@
     def _():
         w_wait(w_recv_sem, W_CORE, 48 * 8)
         size = coupling_t.shape[0]
-        high, low = split(coupling_t[...])
-        weights[0:size] = high
-        weights[size : 2 * size] = low
-        weights[2 * size : 3 * size] = high
+        r = lax.broadcasted_iota(jnp.int32, (block, 1), 0)
+        crossing = r // 12 % 2 != lo
+        for parity in range(2):
+            swap = crossing & ((lo + parity) % 2 == 0)
+            for n in range(8):
+                mine = coupling_t[n * block : (n + 1) * block]
+                twin = coupling_t[(n ^ 1) * block : (n ^ 1) * block + block]
+                high, low = split(jnp.where(swap, twin, mine))
+                weights[parity, n * block : (n + 1) * block] = high
+                weights[parity, size + n * block : size + (n + 1) * block] = low
+                weights[parity, 2 * size + n * block : 2 * size + (n + 1) * block] = high
 
     chunk_m = step - LAG_MATMUL
     last = out_hbm.shape[0] - (chunks - 1) * width
@@ -295,14 +324,10 @@
             store_sem.at[chunk % 2],
         )
 
+    by_parity(last_stage, chunk_m)
+
     @pl.when(chunk_m >= 0)
     def _():
-        arrived(FAR_HIGH, chunk_m, half)
-        arrived(EDGE_LOW, chunk_m, cut)
-        arrived(EDGE_HIGH, chunk_m, cut)
-        arrived(EDGE_FAR, chunk_m, cut)
-        arrived(MIXFAR_LOW, chunk_m, mixed // 2)
-        arrived(MIXFAR_HIGH, chunk_m, mixed // 2)
         size = panel.shape[0]
         high, low = split(panel[:, lanes(chunk_m)].T)
         factors[:, 0:size] = high
@@ -315,7 +340,7 @@
             store(chunk_m - 2, width).wait()
 
         results[slot] = residual_ref[...] + jnp.dot(
-            factors[...], weights[...], preferred_element_type=F32
+            factors[...], weights[slot], preferred_element_type=F32
         )
 
         @pl.when(chunk_m < chunks - 1)
@@ -333,11 +358,14 @@
         everything = pl.ds(0, chunks * width)
         ref = incoming.at[pl.ds(0, 15), pl.ds(0, 6), everything]
         pltpu.make_async_copy(ref, ref, send_sem.at[REGROUP]).wait()
-        counts = {ACROSS: block, LOW: block, HIGH: block, FAR_LOW: half, FAR_HIGH: half}
-        counts |= {MIX_LOW: mixed, MIX_HIGH: mixed, EDGE_LOW: cut, EDGE_HIGH: cut, EDGE_FAR: cut}
-        counts |= {MIXFAR_LOW: mixed // 2, MIXFAR_HIGH: mixed // 2}
+        edge, low = sum(cuts), sum(lows)
+        counts = {ACROSS: 2 * block, LOW: 2 * block, HIGH: 2 * block}
+        counts |= {FAR_LOW: 2 * half, FAR_HIGH: 2 * half}
+        counts |= {EDGE_LOW: edge, EDGE_HIGH: edge, EDGE_FAR: edge}
+        counts |= {MIX_LOW: 2 * block - edge, MIX_HIGH: 2 * block - edge}
+        counts |= {MIXFAR_LOW: low, MIXFAR_HIGH: 2 * block - edge - low}
         for kind, count in counts.items():
-            ref = panel.at[pl.ds(0, count), everything]
+            ref = panel.at[pl.ds(0, count), pl.ds(0, chunks // 2 * width)]
             pltpu.make_async_copy(ref, ref, send_sem.at[kind]).wait()
         w_wait(w_send_sem, W_ACROSS, 48)
         w_wait(w_send_sem, W_ALONG, 48 * 6)
@@ -385,7 +413,7 @@
             pltpu.VMEM((16, 8, padded), F32),
             pltpu.VMEM((depth, padded), F32),
             pltpu.VMEM((depth, local_rows), F32),
-            pltpu.VMEM((3 * depth, local_rows), BF16),
+            pltpu.VMEM((2, 3 * depth, local_rows), BF16),
             pltpu.VMEM((LANES, 3 * depth), BF16),
             pltpu.VMEM((2, LANES, local_rows), F32),
             pltpu.SemaphoreType.DMA((2,)),

time: 112 us -> 110 us (0.982)
  Pallas kernels: 106 us -> 104 us
    pallas_call x1, Pallas kernels: 106 us -> 104 us  [shards(): pl.pallas_call(functools.partial(kernel, chunks), grid=(steps,), out_shap...]
where the time goes in v5:
time: 110 us; the launch traced here: 109 us
  Pallas kernels  104 us (95%)
  local copies, waits for them, and re-layouts  4.68 us (4%)
    pallas_call x1, Pallas kernels, shards(): pl.pallas_call(functools.partial(kernel, chunks), grid=(steps,), out_shap...  104 us
    unnamed x1, local copies, waits for them, and re-layouts  4.68 us

profile of v5, /device:TPU:24, one launch (start us, length us, event | category | flops | bytes accessed | tf_op | source)
XLA Modules:
  0.0 108.9 jit_solution(14664107900633819441)
XLA Ops:
  0.0 104.2 %shard_map.55 = f32[4000,768]{1,0:T(8,128)S(1)} custom-call(s32[1,80]{1,0:T(1,128)} %bitcast.9, s32[800]{0:T(1024)} %virtual_ref.1, f32[80,4800]{1,0:T(8,128)} %amps_hbm.1, f32[48,768]{1,0:T(8,128)} %bitcast.8, f32[4000,768]{1,0:T(8,128)} %bitcast.7), custom_call_target="tpu_custom_call" | custom-call | flops 14155776000 | bytes 24576000 | tf_op jit(solution)/shard_map/pallas_call | solution.py:394
  104.2 4.7 %copy.7 = f32[768,4000]{0,1:T(8,128)} copy(f32[768,4000]{0,1:T(8,128)S(1)} %bitcast.6) | data formatting | bytes 24576000

commit v6 on v5

--- a/solution.py
+++ b/solution.py
@@ -13,7 +13,7 @@
 
 LANES = 512
 LAG_REGROUP = 0
-CUT_EVEN = 32
+CUT_EVEN = 40
 CUT_ODD = 40
 LAG_FIRST = 1
 LAG_SECOND = 2

time: 110 us -> 109 us (level)
    pallas_call x1, Pallas kernels: 104 us -> 103 us  [shards(): pl.pallas_call(functools.partial(kernel, chunks), grid=(steps,), out_shap...]
where the time goes in v6:
time: 109 us; the launch traced here: 107 us
  Pallas kernels  103 us (94%)
  local copies, waits for them, and re-layouts  4.68 us (4%)
    pallas_call x1, Pallas kernels, shards(): pl.pallas_call(functools.partial(kernel, chunks), grid=(steps,), out_shap...  103 us
    unnamed x1, local copies, waits for them, and re-layouts  4.68 us

profile of v6, /device:TPU:24, one launch (start us, length us, event | category | flops | bytes accessed | tf_op | source)
XLA Modules:
  0.0 107.3 jit_solution(5217404754448627570)
XLA Ops:
  0.0 102.7 %shard_map.55 = f32[4000,768]{1,0:T(8,128)S(1)} custom-call(s32[1,80]{1,0:T(1,128)} %bitcast.9, s32[800]{0:T(1024)} %virtual_ref.1, f32[80,4800]{1,0:T(8,128)} %amps_hbm.1, f32[48,768]{1,0:T(8,128)} %bitcast.8, f32[4000,768]{1,0:T(8,128)} %bitcast.7), custom_call_target="tpu_custom_call" | custom-call | flops 14155776000 | bytes 24576000 | tf_op jit(solution)/shard_map/pallas_call | solution.py:394
  102.7 4.7 %copy.7 = f32[768,4000]{0,1:T(8,128)} copy(f32[768,4000]{0,1:T(8,128)S(1)} %bitcast.6) | data formatting | bytes 24576000

commit v7 on v6

--- a/solution.py
+++ b/solution.py
@@ -14,7 +14,7 @@
 LANES = 512
 LAG_REGROUP = 0
 CUT_EVEN = 40
-CUT_ODD = 40
+CUT_ODD = 48
 LAG_FIRST = 1
 LAG_SECOND = 2
 LAG_MATMUL = 3

time: 109 us -> 113 us (1.037)
  Pallas kernels: 103 us -> 106 us
    pallas_call x1, Pallas kernels: 103 us -> 106 us  [shards(): pl.pallas_call(functools.partial(kernel, chunks), grid=(steps,), out_shap...]
where the time goes in v7:
time: 113 us; the launch traced here: 111 us
  Pallas kernels  106 us (94%)
  local copies, waits for them, and re-layouts  4.68 us (4%)
    pallas_call x1, Pallas kernels, shards(): pl.pallas_call(functools.partial(kernel, chunks), grid=(steps,), out_shap...  106 us
    unnamed x1, local copies, waits for them, and re-layouts  4.68 us

profile of v7, /device:TPU:24, one launch (start us, length us, event | category | flops | bytes accessed | tf_op | source)
XLA Modules:
  0.0 110.9 jit_solution(17707726800727904627)
XLA Ops:
  0.0 106.3 %shard_map.55 = f32[4000,768]{1,0:T(8,128)S(1)} custom-call(s32[1,80]{1,0:T(1,128)} %bitcast.9, s32[800]{0:T(1024)} %virtual_ref.1, f32[80,4800]{1,0:T(8,128)} %amps_hbm.1, f32[48,768]{1,0:T(8,128)} %bitcast.8, f32[4000,768]{1,0:T(8,128)} %bitcast.7), custom_call_target="tpu_custom_call" | custom-call | flops 14155776000 | bytes 24576000 | tf_op jit(solution)/shard_map/pallas_call | solution.py:394
  106.3 4.7 %copy.7 = f32[768,4000]{0,1:T(8,128)} copy(f32[768,4000]{0,1:T(8,128)S(1)} %bitcast.6) | data formatting | bytes 24576000
